TPU v7x, 32 devices: a whole 2x2x4 slice. The times are simulated.
32 devices in a mesh: parts: 2 (over y), seq: 4 (over z), head: 2 (over x), sub: 2 (over core).
Axes of the slice: x: 2, y: 2, z: 4, core: 2. Of those that a mesh axis runs over, the one named last changes fastest.
Arguments:
- queries: bfloat16 [2560, 4096], P(('parts', 'seq', 'sub'), 'head'), parts along dimension 0, may hold values from -256 to 256
- keys: bfloat16 [2560, 4096], P(('parts', 'seq', 'sub'), 'head'), parts along dimension 0, may hold values from -8 to 8
- values: bfloat16 [2560, 4096], P(('parts', 'seq', 'sub'), 'head'), parts along dimension 0, may hold values from -6 to 6
- bank: float32 [512, 128], replicated, may hold values from -6 to 6
- seeds: int32 [8, 32, 8], P('parts', 'head'), parts along dimension 0, may hold values from 0 to 511
- reach: int32 [64], P(('parts', 'head')), parts along dimension 0, may hold values from 1 to 8, as said below
Outputs:
- attended: bfloat16 [2560, 4096], P(('parts', 'seq', 'sub'), 'head'), parts along dimension 0
There are 2 independent parts, one for each index of `parts`. A program takes and returns all parts, laid end to end along the dimension named above; an argument that names none is the same for every part. Nothing has to cross between parts.
Inputs may be any that keep to these rules, and one draw needn't show every extreme that they name: `reach`: some head has 8 and some head has 1.
All inputs are finite; a program needn't handle non-finite values.
Results may differ from a plain program's by a relative error of at most 0.0064.
Values may be sent and summed in bfloat16 or wider, within the bound.
A program may use at most 64 MiB of HBM per device.

v0:
```python
import jax
import jax.numpy as jnp
from jax import lax
from jax.sharding import PartitionSpec as P

WINDOW = 8


def shifted(shard, axis, by):
    size = lax.axis_size(axis)
    pairs = [(i, i + by) for i in range(size) if 0 <= i + by < size]
    return lax.ppermute(shard, axis, pairs)


def reflect(vectors):
    width = vectors.shape[1]

    def apply_one(matrix, vector):
        image = jnp.dot(matrix, vector, precision=lax.Precision.HIGHEST)
        factor = 2.0 / (jnp.sum(vector * vector) + 1e-06)
        return (matrix - factor * jnp.outer(image, vector), None)

    start = jnp.eye(width, dtype=jnp.float32)
    result, ignored = lax.scan(apply_one, start, vectors)
    return result


def shard_transform(seeds, bank, shard):
    picked = lax.dynamic_index_in_dim(seeds, shard, 0, keepdims=False)
    one_hot = (picked[..., None] == jnp.arange(bank.shape[0], dtype=jnp.int32)).astype(jnp.float32)
    vectors = jnp.einsum("hrb,bx->hrx", one_hot, bank, precision=lax.Precision.HIGHEST)
    return jax.vmap(reflect)(vectors)


def rotate(walked, transform):
    return jnp.einsum(
        "thx,hxy->thy", walked.astype(jnp.float32), transform, precision=lax.Precision.HIGHEST
    ).astype(jnp.bfloat16)


def attend_block(query_heads, key_heads, value_heads, allowed, scale):
    scores = (
        jnp.einsum("thx,khx->htk", query_heads, key_heads, preferred_element_type=jnp.float32)
        * scale
    )
    if allowed is not None:
        scores = jnp.where(allowed[None], scores, -1e30)
    peak = jnp.max(scores, axis=-1)
    exp_terms = jnp.exp(scores - peak[..., None])
    total = jnp.sum(exp_terms, axis=-1)
    weights = exp_terms.astype(jnp.bfloat16)
    summed = jnp.einsum("htk,khx->thx", weights, value_heads, preferred_element_type=jnp.float32)
    output = (summed / jnp.transpose(total)[..., None]).astype(jnp.bfloat16)
    return (output, jnp.transpose(peak), jnp.transpose(total))


def weigh(output, peak, total, live):
    peak = jnp.where(live[None, :], peak, -1e30)
    total = total * live.astype(jnp.float32)[None, :]
    return (total[..., None] * output.astype(jnp.float32), peak, total)


def combine(first, second):
    highest = jnp.maximum(first[1], second[1])
    scale_one = jnp.exp(first[1] - highest)
    scale_two = jnp.exp(second[1] - highest)
    summed = first[0] * scale_one[..., None] + second[0] * scale_two[..., None]
    return (summed, highest, first[2] * scale_one + second[2] * scale_two)


def shards(queries, keys, values, bank, seeds, reach):
    length = queries.shape[0]
    head_count = reach.shape[0]
    width = queries.shape[1] // head_count
    scale = width ** (-0.5)
    here = lax.axis_index("seq")
    half = lax.axis_index("sub")
    query_heads = queries.reshape(length, head_count, width)
    key_whole, value_whole = (
        lax.all_gather(keys, "sub", axis=0, tiled=True),
        lax.all_gather(values, "sub", axis=0, tiled=True),
    )
    key_heads = key_whole.reshape(2 * length, head_count, width)
    value_heads = value_whole.reshape(2 * length, head_count, width)
    query_places = half * length + jnp.arange(length, dtype=jnp.int32)
    key_places = jnp.arange(2 * length, dtype=jnp.int32)
    causal = query_places[:, None] >= key_places[None, :]
    output, peak, total = attend_block(query_heads, key_heads, value_heads, causal, scale)
    state = (total[..., None] * output.astype(jnp.float32), peak, total)
    key_moving, value_moving = (key_whole, value_whole)
    walked = query_heads
    for distance in range(1, WINDOW + 1):
        source = jnp.maximum(here - distance + 1, 0)
        walked = rotate(walked, shard_transform(seeds, bank, source))
        key_moving, value_moving = shifted((key_moving, value_moving), "seq", 1)
        output, peak, total = attend_block(
            walked,
            key_moving.reshape(2 * length, head_count, width),
            value_moving.reshape(2 * length, head_count, width),
            None,
            scale,
        )
        live = (reach >= distance) & (here >= distance)
        state = combine(state, weigh(output, peak, total, live))
    result = (state[0] / state[2][..., None]).astype(jnp.bfloat16)
    return result.reshape(length, head_count * width)


def solution(mesh):
    return jax.shard_map(
        shards,
        mesh=mesh,
        in_specs=(
            P(("parts", "seq", "sub"), "head"),
            P(("parts", "seq", "sub"), "head"),
            P(("parts", "seq", "sub"), "head"),
            P(),
            P("parts", "head", None),
            P(("parts", "head")),
        ),
        out_specs=P(("parts", "seq", "sub"), "head"),
        check_vma=False,
    )
```

profile of v0, /device:TPU:24, one launch (start us, length us, event | category | flops | bytes accessed | tf_op | source)
XLA Modules:
  0.0 709.9 jit_solution(3945621383320693179)
XLA Ops:
  8.7 20.6 %while.87 = (s32[]{:T(128)}, f32[16,128,128]{2,1,0:T(8,128)S(1)}, f32[8,16,128]{2,1,0:T(8,128)S(1)}, s32[]{:T(128)}) while((s32[]{:T(128)}, f32[16,128,128]{2,1,0:T(8,128)S(1)}, f32[8,16,128]{2,1,0:T(8,128)S(1)}, s32[]{:T(128)}) %tuple.197), condition=%wide.region_39.40_spmd, body=%wide.region_37.39_spmd.sunk | while | flops 3936274 | bytes 3195201 | solution.py:24
  29.8 20.6 %while.86 = (s32[]{:T(128)}, f32[16,128,128]{2,1,0:T(8,128)S(1)}, f32[8,16,128]{2,1,0:T(8,128)S(1)}, s32[]{:T(128)}) while((s32[]{:T(128)}, f32[16,128,128]{2,1,0:T(8,128)S(1)}, f32[8,16,128]{2,1,0:T(8,128)S(1)}, s32[]{:T(128)}) %tuple.200), condition=%wide.region_34.35_spmd, body=%wide.region_32.34_spmd.sunk | while | flops 3936274 | bytes 3195201 | solution.py:24
  52.0 38.4 %while.85 = (s32[]{:T(128)}, f32[16,128,128]{2,1,0:T(8,128)}, f32[8,16,128]{2,1,0:T(8,128)S(1)}, s32[]{:T(128)}) while((s32[]{:T(128)}, f32[16,128,128]{2,1,0:T(8,128)}, f32[8,16,128]{2,1,0:T(8,128)S(1)}, s32[]{:T(128)}) %tuple.203), condition=%wide.region_29.30_spmd, body=%wide.region_27.29_spmd.sunk | while | flops 3936274 | bytes 11583865 | solution.py:24
  52.1 3.0 fusion.349
  56.9 3.0 fusion.349
  61.7 3.0 fusion.349
  66.5 3.0 fusion.349
  91.0 20.6 %while.84 = (s32[]{:T(128)}, f32[16,128,128]{2,1,0:T(8,128)S(1)}, f32[8,16,128]{2,1,0:T(8,128)S(1)}, s32[]{:T(128)}) while((s32[]{:T(128)}, f32[16,128,128]{2,1,0:T(8,128)S(1)}, f32[8,16,128]{2,1,0:T(8,128)S(1)}, s32[]{:T(128)}) %tuple.206), condition=%wide.region_24.25_spmd, body=%wide.region_22.24_spmd.sunk | while | flops 3936274 | bytes 3195201 | solution.py:24
  113.2 39.1 %while.83 = (s32[]{:T(128)}, f32[16,128,128]{2,1,0:T(8,128)}, f32[8,16,128]{2,1,0:T(8,128)S(1)}, s32[]{:T(128)}) while((s32[]{:T(128)}, f32[16,128,128]{2,1,0:T(8,128)}, f32[8,16,128]{2,1,0:T(8,128)S(1)}, s32[]{:T(128)}) %tuple.209), condition=%wide.region_19.20_spmd, body=%wide.region_17.19_spmd.sunk | while | flops 3936274 | bytes 11583865 | solution.py:24
  113.3 3.0 fusion.343
  152.9 21.0 %while.82 = (s32[]{:T(128)}, f32[16,128,128]{2,1,0:T(8,128)S(1)}, f32[8,16,128]{2,1,0:T(8,128)S(1)}, s32[]{:T(128)}) while((s32[]{:T(128)}, f32[16,128,128]{2,1,0:T(8,128)S(1)}, f32[8,16,128]{2,1,0:T(8,128)S(1)}, s32[]{:T(128)}) %tuple.212), condition=%wide.region_14.15_spmd, body=%wide.region_12.14_spmd.sunk | while | flops 3936274 | bytes 3195201 | solution.py:24
  175.5 38.4 %while.81 = (s32[]{:T(128)}, f32[16,128,128]{2,1,0:T(8,128)}, f32[8,16,128]{2,1,0:T(8,128)S(1)}, s32[]{:T(128)}) while((s32[]{:T(128)}, f32[16,128,128]{2,1,0:T(8,128)}, f32[8,16,128]{2,1,0:T(8,128)S(1)}, s32[]{:T(128)}) %tuple.215), condition=%wide.region_9.10_spmd, body=%wide.region_7.9_spmd.sunk | while | flops 3936274 | bytes 11583865 | solution.py:24
  175.6 3.0 fusion.337
  185.2 3.0 fusion.337
  214.5 20.6 %while.80 = (s32[]{:T(128)}, f32[16,128,128]{2,1,0:T(8,128)S(1)}, f32[8,16,128]{2,1,0:T(8,128)S(1)}, s32[]{:T(128)}) while((s32[]{:T(128)}, f32[16,128,128]{2,1,0:T(8,128)S(1)}, f32[8,16,128]{2,1,0:T(8,128)S(1)}, s32[]{:T(128)}) %tuple.218), condition=%wide.region_4.5_spmd, body=%wide.region_2.4_spmd.sunk | while | flops 3936274 | bytes 3195201 | solution.py:24
  246.4 24.1 %collective-permute-done = bf16[320,2048]{1,0:T(8,128)(2,1)} collective-permute-done((bf16[320,2048]{1,0:T(8,128)(2,1)}, bf16[320,2048]{1,0:T(8,128)(2,1)}, u32[]{:S(2)}, u32[]{:S(2)}) %collective-permute-start) | collective-permute-done | bytes 1310752 | tf_op jit(solution)/shard_map/ppermute | solution.py:12
  271.9 26.6 %collective-permute-done.1 = bf16[320,2048]{1,0:T(8,128)(2,1)S(1)} collective-permute-done((bf16[320,2048]{1,0:T(8,128)(2,1)}, bf16[320,2048]{1,0:T(8,128)(2,1)S(1)}, u32[]{:S(2)}, u32[]{:S(2)}) %collective-permute-start.1) | collective-permute-done | bytes 1310752 | tf_op jit(solution)/shard_map/ppermute | solution.py:12
  303.1 23.5 %collective-permute-done.2 = bf16[320,2048]{1,0:T(8,128)(2,1)S(1)} collective-permute-done((bf16[320,2048]{1,0:T(8,128)(2,1)}, bf16[320,2048]{1,0:T(8,128)(2,1)S(1)}, u32[]{:S(2)}, u32[]{:S(2)}) %collective-permute-start.2) | collective-permute-done | bytes 1310752 | tf_op jit(solution)/shard_map/ppermute | solution.py:12
  329.5 25.2 %collective-permute-done.3 = bf16[320,2048]{1,0:T(8,128)(2,1)S(1)} collective-permute-done((bf16[320,2048]{1,0:T(8,128)(2,1)S(1)}, bf16[320,2048]{1,0:T(8,128)(2,1)S(1)}, u32[]{:S(2)}, u32[]{:S(2)}) %collective-permute-start.3) | collective-permute-done | bytes 1310752 | tf_op jit(solution)/shard_map/ppermute | solution.py:12
  361.2 21.6 %collective-permute-done.4 = bf16[320,2048]{1,0:T(8,128)(2,1)S(1)} collective-permute-done((bf16[320,2048]{1,0:T(8,128)(2,1)S(1)}, bf16[320,2048]{1,0:T(8,128)(2,1)S(1)}, u32[]{:S(2)}, u32[]{:S(2)}) %collective-permute-start.4) | collective-permute-done | bytes 1310752 | tf_op jit(solution)/shard_map/ppermute | solution.py:12
  385.5 25.4 %collective-permute-done.5 = bf16[320,2048]{1,0:T(8,128)(2,1)S(1)} collective-permute-done((bf16[320,2048]{1,0:T(8,128)(2,1)S(1)}, bf16[320,2048]{1,0:T(8,128)(2,1)S(1)}, u32[]{:S(2)}, u32[]{:S(2)}) %collective-permute-start.5) | collective-permute-done | bytes 1310752 | tf_op jit(solution)/shard_map/ppermute | solution.py:12
  415.8 23.1 %collective-permute-done.6 = bf16[320,2048]{1,0:T(8,128)(2,1)S(1)} collective-permute-done((bf16[320,2048]{1,0:T(8,128)(2,1)S(1)}, bf16[320,2048]{1,0:T(8,128)(2,1)S(1)}, u32[]{:S(2)}, u32[]{:S(2)}) %collective-permute-start.6) | collective-permute-done | bytes 1310752 | tf_op jit(solution)/shard_map/ppermute | solution.py:12
  441.3 25.7 %collective-permute-done.7 = bf16[320,2048]{1,0:T(8,128)(2,1)S(1)} collective-permute-done((bf16[320,2048]{1,0:T(8,128)(2,1)S(1)}, bf16[320,2048]{1,0:T(8,128)(2,1)S(1)}, u32[]{:S(2)}, u32[]{:S(2)}) %collective-permute-start.7) | collective-permute-done | bytes 1310752 | tf_op jit(solution)/shard_map/ppermute | solution.py:12
  472.0 23.1 %collective-permute-done.8 = bf16[320,2048]{1,0:T(8,128)(2,1)S(1)} collective-permute-done((bf16[320,2048]{1,0:T(8,128)(2,1)S(1)}, bf16[320,2048]{1,0:T(8,128)(2,1)S(1)}, u32[]{:S(2)}, u32[]{:S(2)}) %collective-permute-start.8) | collective-permute-done | bytes 1310752 | tf_op jit(solution)/shard_map/ppermute | solution.py:12
  497.8 25.4 %collective-permute-done.9 = bf16[320,2048]{1,0:T(8,128)(2,1)S(1)} collective-permute-done((bf16[320,2048]{1,0:T(8,128)(2,1)S(1)}, bf16[320,2048]{1,0:T(8,128)(2,1)S(1)}, u32[]{:S(2)}, u32[]{:S(2)}) %collective-permute-start.9) | collective-permute-done | bytes 1310752 | tf_op jit(solution)/shard_map/ppermute | solution.py:12
  528.2 23.2 %collective-permute-done.10 = bf16[320,2048]{1,0:T(8,128)(2,1)S(1)} collective-permute-done((bf16[320,2048]{1,0:T(8,128)(2,1)S(1)}, bf16[320,2048]{1,0:T(8,128)(2,1)S(1)}, u32[]{:S(2)}, u32[]{:S(2)}) %collective-permute-start.10) | collective-permute-done | bytes 1310752 | tf_op jit(solution)/shard_map/ppermute | solution.py:12
  554.0 25.4 %collective-permute-done.11 = bf16[320,2048]{1,0:T(8,128)(2,1)S(1)} collective-permute-done((bf16[320,2048]{1,0:T(8,128)(2,1)S(1)}, bf16[320,2048]{1,0:T(8,128)(2,1)S(1)}, u32[]{:S(2)}, u32[]{:S(2)}) %collective-permute-start.11) | collective-permute-done | bytes 1310752 | tf_op jit(solution)/shard_map/ppermute | solution.py:12
  584.6 22.9 %collective-permute-done.12 = bf16[320,2048]{1,0:T(8,128)(2,1)S(1)} collective-permute-done((bf16[320,2048]{1,0:T(8,128)(2,1)S(1)}, bf16[320,2048]{1,0:T(8,128)(2,1)S(1)}, u32[]{:S(2)}, u32[]{:S(2)}) %collective-permute-start.12) | collective-permute-done | bytes 1310752 | tf_op jit(solution)/shard_map/ppermute | solution.py:12
  608.9 26.7 %collective-permute-done.13 = bf16[320,2048]{1,0:T(8,128)(2,1)S(1)} collective-permute-done((bf16[320,2048]{1,0:T(8,128)(2,1)S(1)}, bf16[320,2048]{1,0:T(8,128)(2,1)S(1)}, u32[]{:S(2)}, u32[]{:S(2)}) %collective-permute-start.13) | collective-permute-done | bytes 1310752 | tf_op jit(solution)/shard_map/ppermute | solution.py:12
  640.5 23.1 %collective-permute-done.14 = bf16[320,2048]{1,0:T(8,128)(2,1)S(1)} collective-permute-done((bf16[320,2048]{1,0:T(8,128)(2,1)S(1)}, bf16[320,2048]{1,0:T(8,128)(2,1)S(1)}, u32[]{:S(2)}, u32[]{:S(2)}) %collective-permute-start.14) | collective-permute-done | bytes 1310752 | tf_op jit(solution)/shard_map/ppermute | solution.py:12
  666.1 24.5 %collective-permute-done.15 = bf16[320,2048]{1,0:T(8,128)(2,1)S(1)} collective-permute-done((bf16[320,2048]{1,0:T(8,128)(2,1)S(1)}, bf16[320,2048]{1,0:T(8,128)(2,1)S(1)}, u32[]{:S(2)}, u32[]{:S(2)}) %collective-permute-start.15) | collective-permute-done | bytes 1310752 | tf_op jit(solution)/shard_map/ppermute | solution.py:12
  690.6 11.0 %fusion.145 = bf16[16,20,8,128]{3,2,1,0:T(8,128)(2,1)S(1)} fusion(f32[16,160,320]{2,1,0:T(8,128)S(1)} %get-tuple-element.280, f32[16,160]{1,0:T(8,128)S(1)} %get-tuple-element.279, bf16[160,16,128]{2,0,1:T(8,128)(2,1)S(1)} %divide_convert_fusion.2, bf16[160,16,128]{2,0,1:T(8,128)(2,1)S(1)} %divide_convert_fusion.3, ...), kind=kOutput, calls=%fused_computation.186 | convolution fusion | flops 227246080 | bytes 10772480 | tf_op jit(solution)/shard_map/htk,khx->thx/dot_general | solution.py:52
  (471 shorter events, 271.6 us)
Async XLA Ops:
  6.5 228.5 %copy-start = (bf16[160,2048]{1,0:T(8,128)(2,1)S(1)}, bf16[160,2048]{1,0:T(8,128)(2,1)}, u32[]{:S(2)}) copy-start(bf16[160,2048]{1,0:T(8,128)(2,1)} %param.22) | copy-start | bytes 1966084
  6.5 230.1 %all-gather.3.cloned.1.call-start = ((), (), s32[]{:S(2)}) async-start(), calls=%async_computation | async-start | bytes 1966080 | tf_op jit(solution)/shard_map/all_gather | solution.py:80
  7.3 232.9 %all-gather.5.cloned.1.call-start = ((), (), s32[]{:S(2)}) async-start(), calls=%async_computation.1 | async-start | bytes 1966080 | tf_op jit(solution)/shard_map/all_gather | solution.py:81
  52.0 3.1 copy-start.4
  66.4 3.1 copy-start.4
  76.0 3.1 copy-start.4
  113.2 3.1 copy-start.9
  123.0 3.1 copy-start.9
  127.9 3.1 copy-start.9
  147.4 3.1 copy-start.9
  175.5 3.1 copy-start.13
  236.7 33.9 %collective-permute-start = (bf16[320,2048]{1,0:T(8,128)(2,1)}, bf16[320,2048]{1,0:T(8,128)(2,1)}, u32[]{:S(2)}, u32[]{:S(2)}) collective-permute-start(bf16[320,2048]{1,0:T(8,128)(2,1)} %all-gather.3.cloned.1.call-done), channel_id=1, source_target_pairs={{0,4},{4,8},{8,12},{1,5},{5,9},{9,13},{2,6},{6,10},{10,14},{3,7},{... | collective-permute-start | bytes 3932168 | tf_op jit(solution)/shard_map/ppermute | solution.py:12
  240.1 3.5 copy-start.11
  240.2 58.3 %collective-permute-start.1 = (bf16[320,2048]{1,0:T(8,128)(2,1)}, bf16[320,2048]{1,0:T(8,128)(2,1)S(1)}, u32[]{:S(2)}, u32[]{:S(2)}) collective-permute-start(bf16[320,2048]{1,0:T(8,128)(2,1)} %all-gather.5.cloned.1.call-done), channel_id=1, source_target_pairs={{0,4},{4,8},{8,12},{1,5},{5,9},{9,13},{2,6},{6,10},{10,14},{3,7},{... | collective-permute-start | bytes 3932168 | tf_op jit(solution)/shard_map/ppermute | solution.py:12
  245.5 54.4 %copy-start.18 = (s32[16]{0:T(128)S(1)}, s32[16]{0:T(128)}, u32[]{:S(2)}) copy-start(s32[16]{0:T(128)} %param.27) | copy-start | bytes 196
  245.6 54.5 %copy-start.3 = (f32[16,128,128]{2,1,0:T(8,128)S(1)}, f32[16,128,128]{2,1,0:T(8,128)}, u32[]{:S(2)}) copy-start(f32[16,128,128]{2,1,0:T(8,128)} %copy-done.2) | copy-start | bytes 3145732
  270.5 56.1 %collective-permute-start.2 = (bf16[320,2048]{1,0:T(8,128)(2,1)}, bf16[320,2048]{1,0:T(8,128)(2,1)S(1)}, u32[]{:S(2)}, u32[]{:S(2)}) collective-permute-start(bf16[320,2048]{1,0:T(8,128)(2,1)} %collective-permute-done), channel_id=1, source_target_pairs={{0,4},{4,8},{8,12},{1,5},{5,9},{9,13},{2,6},{6,10},{10,14},{3,7},{... | collective-permute-start | bytes 3932168 | tf_op jit(solution)/shard_map/ppermute | solution.py:12
  298.5 56.2 %collective-permute-start.3 = (bf16[320,2048]{1,0:T(8,128)(2,1)S(1)}, bf16[320,2048]{1,0:T(8,128)(2,1)S(1)}, u32[]{:S(2)}, u32[]{:S(2)}) collective-permute-start(bf16[320,2048]{1,0:T(8,128)(2,1)S(1)} %collective-permute-done.1), channel_id=1, source_target_pairs={{0,4},{4,8},{8,12},{1,5},{5,9},{9,13},{2,6},{6,10},{10,14},{3,7},{... | collective-permute-start | bytes 3932168 | tf_op jit(solution)/shard_map/ppermute | solution.py:12
  326.6 56.2 %collective-permute-start.4 = (bf16[320,2048]{1,0:T(8,128)(2,1)S(1)}, bf16[320,2048]{1,0:T(8,128)(2,1)S(1)}, u32[]{:S(2)}, u32[]{:S(2)}) collective-permute-start(bf16[320,2048]{1,0:T(8,128)(2,1)S(1)} %collective-permute-done.2), channel_id=1, source_target_pairs={{0,4},{4,8},{8,12},{1,5},{5,9},{9,13},{2,6},{6,10},{10,14},{3,7},{... | collective-permute-start | bytes 3932168 | tf_op jit(solution)/shard_map/ppermute | solution.py:12
  327.9 28.1 %copy-start.19 = (bf16[320,2048]{1,0:T(8,128)(2,1)S(1)}, bf16[320,2048]{1,0:T(8,128)(2,1)}, u32[]{:S(2)}) copy-start(bf16[320,2048]{1,0:T(8,128)(2,1)} %all-gather.5.cloned.1.call-done) | copy-start | bytes 3932164
  354.7 56.2 %collective-permute-start.5 = (bf16[320,2048]{1,0:T(8,128)(2,1)S(1)}, bf16[320,2048]{1,0:T(8,128)(2,1)S(1)}, u32[]{:S(2)}, u32[]{:S(2)}) collective-permute-start(bf16[320,2048]{1,0:T(8,128)(2,1)S(1)} %collective-permute-done.3), channel_id=1, source_target_pairs={{0,4},{4,8},{8,12},{1,5},{5,9},{9,13},{2,6},{6,10},{10,14},{3,7},{... | collective-permute-start | bytes 3932168 | tf_op jit(solution)/shard_map/ppermute | solution.py:12
  382.8 56.2 %collective-permute-start.6 = (bf16[320,2048]{1,0:T(8,128)(2,1)S(1)}, bf16[320,2048]{1,0:T(8,128)(2,1)S(1)}, u32[]{:S(2)}, u32[]{:S(2)}) collective-permute-start(bf16[320,2048]{1,0:T(8,128)(2,1)S(1)} %collective-permute-done.4), channel_id=1, source_target_pairs={{0,4},{4,8},{8,12},{1,5},{5,9},{9,13},{2,6},{6,10},{10,14},{3,7},{... | collective-permute-start | bytes 3932168 | tf_op jit(solution)/shard_map/ppermute | solution.py:12
  410.9 56.2 %collective-permute-start.7 = (bf16[320,2048]{1,0:T(8,128)(2,1)S(1)}, bf16[320,2048]{1,0:T(8,128)(2,1)S(1)}, u32[]{:S(2)}, u32[]{:S(2)}) collective-permute-start(bf16[320,2048]{1,0:T(8,128)(2,1)S(1)} %collective-permute-done.5), channel_id=1, source_target_pairs={{0,4},{4,8},{8,12},{1,5},{5,9},{9,13},{2,6},{6,10},{10,14},{3,7},{... | collective-permute-start | bytes 3932168 | tf_op jit(solution)/shard_map/ppermute | solution.py:12
  439.0 56.2 %collective-permute-start.8 = (bf16[320,2048]{1,0:T(8,128)(2,1)S(1)}, bf16[320,2048]{1,0:T(8,128)(2,1)S(1)}, u32[]{:S(2)}, u32[]{:S(2)}) collective-permute-start(bf16[320,2048]{1,0:T(8,128)(2,1)S(1)} %collective-permute-done.6), channel_id=1, source_target_pairs={{0,4},{4,8},{8,12},{1,5},{5,9},{9,13},{2,6},{6,10},{10,14},{3,7},{... | collective-permute-start | bytes 3932168 | tf_op jit(solution)/shard_map/ppermute | solution.py:12
  467.0 56.2 %collective-permute-start.9 = (bf16[320,2048]{1,0:T(8,128)(2,1)S(1)}, bf16[320,2048]{1,0:T(8,128)(2,1)S(1)}, u32[]{:S(2)}, u32[]{:S(2)}) collective-permute-start(bf16[320,2048]{1,0:T(8,128)(2,1)S(1)} %collective-permute-done.7), channel_id=1, source_target_pairs={{0,4},{4,8},{8,12},{1,5},{5,9},{9,13},{2,6},{6,10},{10,14},{3,7},{... | collective-permute-start | bytes 3932168 | tf_op jit(solution)/shard_map/ppermute | solution.py:12
  495.1 56.2 %collective-permute-start.10 = (bf16[320,2048]{1,0:T(8,128)(2,1)S(1)}, bf16[320,2048]{1,0:T(8,128)(2,1)S(1)}, u32[]{:S(2)}, u32[]{:S(2)}) collective-permute-start(bf16[320,2048]{1,0:T(8,128)(2,1)S(1)} %collective-permute-done.8), channel_id=1, source_target_pairs={{0,4},{4,8},{8,12},{1,5},{5,9},{9,13},{2,6},{6,10},{10,14},{3,7},{... | collective-permute-start | bytes 3932168 | tf_op jit(solution)/shard_map/ppermute | solution.py:12
  523.2 56.2 %collective-permute-start.11 = (bf16[320,2048]{1,0:T(8,128)(2,1)S(1)}, bf16[320,2048]{1,0:T(8,128)(2,1)S(1)}, u32[]{:S(2)}, u32[]{:S(2)}) collective-permute-start(bf16[320,2048]{1,0:T(8,128)(2,1)S(1)} %collective-permute-done.9), channel_id=1, source_target_pairs={{0,4},{4,8},{8,12},{1,5},{5,9},{9,13},{2,6},{6,10},{10,14},{3,7},{... | collective-permute-start | bytes 3932168 | tf_op jit(solution)/shard_map/ppermute | solution.py:12
  551.3 56.2 %collective-permute-start.12 = (bf16[320,2048]{1,0:T(8,128)(2,1)S(1)}, bf16[320,2048]{1,0:T(8,128)(2,1)S(1)}, u32[]{:S(2)}, u32[]{:S(2)}) collective-permute-start(bf16[320,2048]{1,0:T(8,128)(2,1)S(1)} %collective-permute-done.10), channel_id=1, source_target_pairs={{0,4},{4,8},{8,12},{1,5},{5,9},{9,13},{2,6},{6,10},{10,14},{3,7},{... | collective-permute-start | bytes 3932168 | tf_op jit(solution)/shard_map/ppermute | solution.py:12
  579.4 56.2 %collective-permute-start.13 = (bf16[320,2048]{1,0:T(8,128)(2,1)S(1)}, bf16[320,2048]{1,0:T(8,128)(2,1)S(1)}, u32[]{:S(2)}, u32[]{:S(2)}) collective-permute-start(bf16[320,2048]{1,0:T(8,128)(2,1)S(1)} %collective-permute-done.11), channel_id=1, source_target_pairs={{0,4},{4,8},{8,12},{1,5},{5,9},{9,13},{2,6},{6,10},{10,14},{3,7},{... | collective-permute-start | bytes 3932168 | tf_op jit(solution)/shard_map/ppermute | solution.py:12
  607.5 56.2 %collective-permute-start.14 = (bf16[320,2048]{1,0:T(8,128)(2,1)S(1)}, bf16[320,2048]{1,0:T(8,128)(2,1)S(1)}, u32[]{:S(2)}, u32[]{:S(2)}) collective-permute-start(bf16[320,2048]{1,0:T(8,128)(2,1)S(1)} %collective-permute-done.12), channel_id=1, source_target_pairs={{0,4},{4,8},{8,12},{1,5},{5,9},{9,13},{2,6},{6,10},{10,14},{3,7},{... | collective-permute-start | bytes 3932168 | tf_op jit(solution)/shard_map/ppermute | solution.py:12
  635.6 55.0 %collective-permute-start.15 = (bf16[320,2048]{1,0:T(8,128)(2,1)S(1)}, bf16[320,2048]{1,0:T(8,128)(2,1)S(1)}, u32[]{:S(2)}, u32[]{:S(2)}) collective-permute-start(bf16[320,2048]{1,0:T(8,128)(2,1)S(1)} %collective-permute-done.13), channel_id=1, source_target_pairs={{0,4},{4,8},{8,12},{1,5},{5,9},{9,13},{2,6},{6,10},{10,14},{3,7},{... | collective-permute-start | bytes 3932168 | tf_op jit(solution)/shard_map/ppermute | solution.py:12
  690.6 12.0 %copy-start.1 = (bf16[160,2048]{1,0:T(8,128)(2,1)S(1)}, bf16[160,2048]{1,0:T(8,128)(2,1)}, u32[]{:S(2)}) copy-start(bf16[160,2048]{1,0:T(8,128)(2,1)} %param.22) | copy-start | bytes 1966084
  (49 other events, 87.6 us)
Sparse Core Ops, SparseCore 0:
  8.9 10.6 all-gather.2
  21.1 10.5 all-gather.4
where the time goes:
time: 720 us; the launch traced here: 710 us
  waiting for transfers between devices  391 us (54%)
  matrix products  185 us (26%)
  other arithmetic  65.3 us (9%)
  local copies, waits for them, and re-layouts  30.4 us (4%)
  starting transfers between devices  21.3 us (3%)
  between operations  14.5 us (2%)
    ppermute x16, waiting for transfers between devices, shifted(): return lax.ppermute(shard, axis, pairs)  390 us
    dot_general x64, matrix products, apply_one(): image = jnp.dot(matrix, vector, precision=lax.Precision.HIGHEST)  142 us
    sub x64, other arithmetic, apply_one(): return (matrix - factor * jnp.outer(image, vector), None)  43.9 us
    while x96, local copies, waits for them, and re-layouts  23.9 us
    dot_general x9, matrix products, attend_block(): jnp.einsum('htk,khx->thx', weights, value_heads, preferred_element_type=j...  22.5 us
    ppermute x16, starting transfers between devices, shifted(): return lax.ppermute(shard, axis, pairs)  21.3 us
  transfers between devices with their start and end apart: 18, of which 16 were waited for; matrix products, arithmetic and copies ran while one was open for 34% of the time, Pallas kernels for 0%

commit v1 on v0

v1 whole, which is shorter than its diff:
```python
import functools
import math

import jax
import jax.numpy as jnp
from jax import lax
from jax.experimental import pallas as pl
from jax.experimental.pallas import tpu as pltpu
from jax.sharding import PartitionSpec as P

WINDOW = 8
GROUP = 2
LOW = -1e30
NT = (((1,), (1,)), ((), ()))
TN = (((0,), (0,)), ((), ()))
HIGH = lax.Precision.HIGHEST
F32 = jnp.float32
BF16 = jnp.bfloat16
MESH = pl.DeviceIdType.MESH


def split3(x):
    one = x.astype(BF16).astype(F32)
    rest = x - one
    two = rest.astype(BF16).astype(F32)
    return one, two, rest - two


def build_transforms(here, bank_ref, seeds_ref, u_ref, t_ref, heads, refl, width):
    rows = heads * refl

    def pick(h, carry):
        for r in range(refl):
            row = seeds_ref[here, h, r]
            u_ref[pl.ds(h * refl + r, 1), :] = bank_ref[pl.ds(row, 1), :]
        return carry

    lax.fori_loop(0, heads, pick, 0)
    v = u_ref[...]
    u = v * jnp.sqrt(2.0 / (jnp.sum(v * v, axis=1, keepdims=True) + 1e-6))
    gram = lax.dot_general(u, u, NT, precision=HIGH, preferred_element_type=F32)
    row = lax.broadcasted_iota(jnp.int32, (rows, rows), 0)
    col = lax.broadcasted_iota(jnp.int32, (rows, rows), 1)
    gram = jnp.where(row < col, gram, 0.0)
    eye = jnp.where(row == col, 1.0, 0.0).astype(F32)
    inverse = eye - jnp.where(row // 2 == col // 2, gram, 0.0)
    size = 2
    while size < refl:
        cross = jnp.where(
            (row // (2 * size) == col // (2 * size)) & (row // size != col // size), gram, 0.0
        )
        inner = jnp.dot(cross, inverse, precision=HIGH, preferred_element_type=F32)
        inverse = inverse - jnp.dot(inverse, inner, precision=HIGH, preferred_element_type=F32)
        size *= 2
    w = jnp.dot(inverse, u, precision=HIGH, preferred_element_type=F32)
    u1, u2, u3 = split3(u)
    w1, w2, w3 = split3(w)
    wide_row = lax.broadcasted_iota(jnp.int32, (width, width), 0)
    wide_col = lax.broadcasted_iota(jnp.int32, (width, width), 1)
    wide_eye = jnp.where(wide_row == wide_col, 1.0, 0.0).astype(F32)
    for h in range(heads):
        at = slice(h * refl, (h + 1) * refl)
        left = jnp.concatenate([u1[at], u1[at], u1[at], u2[at], u2[at], u3[at]], axis=0)
        right = jnp.concatenate([w1[at], w2[at], w3[at], w1[at], w2[at], w1[at]], axis=0)
        t = wide_eye - lax.dot_general(
            left.astype(BF16), right.astype(BF16), TN, preferred_element_type=F32
        )
        t1, t2, t3 = split3(t)
        t_ref[h] = jnp.concatenate([t1, t2, t3], axis=1).astype(BF16)


def rotate(q, t):
    width = q.shape[1]
    out = jnp.dot(q, t, preferred_element_type=F32)
    return (out[:, :width] + out[:, width : 2 * width] + out[:, 2 * width :]).astype(BF16)


def block(q, k, v, factor, allowed):
    s = lax.dot_general(q, k, NT, preferred_element_type=F32)
    if allowed is not None:
        s = jnp.where(allowed, s, LOW)
    m = jnp.max(s, axis=1, keepdims=True)
    p = jnp.exp2((s - m) * factor)
    total = jnp.sum(p, axis=1, keepdims=True)
    o = jnp.dot(p.astype(BF16), v, preferred_element_type=F32)
    return o, m * factor, total


def gated(state, live):
    o, m, total = state
    return jnp.where(live, o, 0.0), jnp.where(live, m, LOW), jnp.where(live, total, 0.0)


def merge(first, second):
    o1, m1, l1 = first
    o2, m2, l2 = second
    m = jnp.maximum(m1, m2)
    a1 = jnp.exp2(m1 - m)
    a2 = jnp.exp2(m2 - m)
    return o1 * a1 + o2 * a2, m, l1 * a1 + l2 * a2


def kernel(
    n, slots, q_hbm, k_hbm, v_hbm, bank_ref, seeds_ref, reach_ref, out_ref,
    q_ref, kb, vb, k0, v0, u_ref, t_ref, qr, qs, orx, osx, str_, sts, acc, ms, ls,
    load_sem, ex_send, ex_recv, kv_send, kv_recv, re_send, re_recv,
    q_send, q_recv, o_send, o_recv, s_send, s_recv,
):
    length, columns = q_ref.shape
    heads, refl = seeds_ref.shape[1:]
    width = columns // heads
    chunks = heads // GROUP
    wide = GROUP * width
    factor = width ** (-0.5) * math.log2(math.e)
    here = lax.axis_index("seq")
    half = lax.axis_index("sub")
    partner = {"sub": 1 - half}
    below = {"seq": here - 1}
    above = {"seq": here + 1}
    rows = pl.ds(pl.multiple_of(half * length, length), length)
    reached = jnp.where(here >= 1, jnp.minimum(slots, n - 1 - here), 0)

    def cols(g):
        return pl.ds(pl.multiple_of(g * wide, wide), wide)

    def head_cols(h):
        return pl.ds(pl.multiple_of(h * width, width), width)

    loads = [
        pltpu.make_async_copy(q_hbm, q_ref, load_sem.at[0]),
        pltpu.make_async_copy(k_hbm, kb.at[rows, :], load_sem.at[1]),
        pltpu.make_async_copy(v_hbm, vb.at[rows, :], load_sem.at[2]),
    ]
    for c in loads:
        c.start()

    barrier = pltpu.get_barrier_semaphore()
    pl.semaphore_signal(barrier, inc=1, device_id=partner, device_id_type=MESH)

    @pl.when(here > 0)
    def _():
        pl.semaphore_signal(barrier, inc=1, device_id=below, device_id_type=MESH)

    @pl.when(here < n - 1)
    def _():
        pl.semaphore_signal(barrier, inc=1, device_id=above, device_id_type=MESH)

    pl.semaphore_wait(
        barrier, 1 + jnp.where(here > 0, 1, 0) + jnp.where(here < n - 1, 1, 0)
    )

    def exchange(i):
        src, dst = ((k_hbm, kb), (v_hbm, vb))[i]
        return pltpu.make_async_remote_copy(
            src_ref=src, dst_ref=dst.at[rows, :], send_sem=ex_send.at[i],
            recv_sem=ex_recv.at[i], device_id=partner, device_id_type=MESH)

    def first_kv(i, g):
        src, dst = ((k_hbm, k0), (v_hbm, v0))[i]
        return pltpu.make_async_remote_copy(
            src_ref=src.at[:, cols(g)], dst_ref=dst.at[rows, cols(g)],
            send_sem=kv_send.at[i, g], recv_sem=kv_recv.at[i, g],
            device_id=above, device_id_type=MESH)

    def relay(i, g):
        buf = (k0, v0)[i]
        return pltpu.make_async_remote_copy(
            src_ref=buf.at[rows, cols(g)], dst_ref=buf.at[rows, cols(g)],
            send_sem=re_send.at[i, g], recv_sem=re_recv.at[i, g],
            device_id=partner, device_id_type=MESH)

    def send_q(slot, g):
        return pltpu.make_async_remote_copy(
            src_ref=qs.at[slot, :, cols(g)], dst_ref=qr.at[slot, :, cols(g)],
            send_sem=q_send.at[slot, g], recv_sem=q_recv.at[slot, g],
            device_id=below, device_id_type=MESH)

    def send_o(slot, g):
        return pltpu.make_async_remote_copy(
            src_ref=osx.at[slot, :, cols(g)], dst_ref=orx.at[slot, :, cols(g)],
            send_sem=o_send.at[slot, g], recv_sem=o_recv.at[slot, g],
            device_id=above, device_id_type=MESH)

    def send_s(slot, g):
        return pltpu.make_async_remote_copy(
            src_ref=sts.at[slot, g], dst_ref=str_.at[slot, g],
            send_sem=s_send.at[slot, g], recv_sem=s_recv.at[slot, g],
            device_id=above, device_id_type=MESH)

    def loop(count, body):
        def step(i, carry):
            body(i)
            return carry
        lax.fori_loop(0, count, step, 0)

    exchange(0).start()
    exchange(1).start()

    @pl.when(here == 0)
    def _():
        def go(g):
            first_kv(0, g).start()
            first_kv(1, g).start()
        loop(chunks, go)

    for c in loads:
        c.wait()

    @pl.when(here >= 1)
    def _():
        build_transforms(here, bank_ref, seeds_ref, u_ref, t_ref, heads, refl, width)

    @pl.when(here >= 2)
    def _():
        def walk(g):
            for j in range(GROUP):
                h = g * GROUP + j
                qs[0, :, head_cols(h)] = rotate(q_ref[:, head_cols(h)], t_ref[h])
            send_q(0, g).start()

            def onward(i):
                send_q(i, g).wait_recv()

                @pl.when(i + 1 < slots)
                def _():
                    for j in range(GROUP):
                        h = g * GROUP + j
                        qs[i + 1, :, head_cols(h)] = rotate(qr[i, :, head_cols(h)], t_ref[h])
                    send_q(i + 1, g).start()
            loop(reached, onward)
        loop(chunks, walk)

    exchange(0).wait_recv()
    exchange(1).wait_recv()

    place = half * length + lax.broadcasted_iota(jnp.int32, (length, 2 * length), 0)
    allowed = place >= lax.broadcasted_iota(jnp.int32, (length, 2 * length), 1)

    def own(g):
        for j in range(GROUP):
            h = g * GROUP + j
            at = head_cols(h)
            o, m, total = block(q_ref[:, at], kb[:, at], vb[:, at], factor, allowed)
            acc[:, at] = o
            ms[h] = m
            ls[h] = total
    loop(chunks, own)

    def finish(h, state):
        o, m, total = state
        out_ref[:, head_cols(h)] = (o / total).astype(BF16)

    def give(slot, g, states):
        lane = lax.broadcasted_iota(jnp.int32, (length, 128), 1)
        packed = jnp.zeros((length, 128), F32)
        for j, (o, m, total) in enumerate(states):
            osx[slot, :, head_cols(g * GROUP + j)] = (o / jnp.maximum(total, 1.0)).astype(BF16)
            packed = jnp.where(lane == 2 * j, m, packed)
            packed = jnp.where(lane == 2 * j + 1, total, packed)
        padded = sts.shape[3]
        packed = jnp.concatenate([packed, jnp.zeros((padded - length, 128), F32)], axis=0)
        sts[slot, g] = packed.T[: sts.shape[2]]
        send_o(slot, g).start()
        send_s(slot, g).start()

    def take(slot, g):
        send_o(slot, g).wait_recv()
        send_s(slot, g).wait_recv()
        stats = str_[slot, g]
        stats = jnp.concatenate(
            [stats, jnp.zeros((128 - stats.shape[0], stats.shape[1]), F32)], axis=0
        ).T[:length]
        states = []
        for j in range(GROUP):
            m = stats[:, 2 * j : 2 * j + 1]
            total = stats[:, 2 * j + 1 : 2 * j + 2]
            o = orx[slot, :, head_cols(g * GROUP + j)].astype(F32) * total
            states.append((o, m, total))
        return states

    @pl.when(here == 0)
    def _():
        def last(g):
            for j in range(GROUP):
                h = g * GROUP + j
                finish(h, (acc[:, head_cols(h)], ms[h], ls[h]))
        loop(chunks, last)

    @pl.when(here == 1)
    def _():
        def pass_on(g):
            for i in range(2):
                first_kv(i, g).wait_recv()
                relay(i, g).start()

        pass_on(0)

        def work(g):
            for i in range(2):
                relay(i, g).wait_recv()
            for j in range(GROUP):
                h = g * GROUP + j
                at = head_cols(h)
                w = rotate(q_ref[:, at], t_ref[h])
                far = gated(block(w, k0[:, at], v0[:, at], factor, None), reach_ref[h] >= 1)
                finish(h, merge((acc[:, at], ms[h], ls[h]), far))

            @pl.when(g + 1 < chunks)
            def _():
                pass_on(g + 1)

            def guest(i):
                if n > 2:
                    send_q(i, g).wait_recv()
                    states = []
                    for j in range(GROUP):
                        h = g * GROUP + j
                        at = head_cols(h)
                        w = qr[i, :, at]
                        near = gated(
                            block(w, kb[:, at], vb[:, at], factor, None), reach_ref[h] >= i + 1
                        )
                        w = rotate(w, t_ref[h])
                        far = gated(
                            block(w, k0[:, at], v0[:, at], factor, None),
                            (reach_ref[h] >= i + 2) & (i + 2 <= WINDOW),
                        )
                        states.append(merge(near, far))
                    give(i, g, states)
            loop(reached, guest)
        loop(chunks, work)

    @pl.when(here >= 2)
    def _():
        def work(g):
            def guest(i):
                states = []
                for j in range(GROUP):
                    h = g * GROUP + j
                    at = head_cols(h)
                    state = block(qr[i, :, at], kb[:, at], vb[:, at], factor, None)
                    o, m, total = gated(state, reach_ref[h] >= i + 1)
                    acc2 = (o, m, total)
                    states.append(acc2)

                if slots > 1:
                    @pl.when(i + 1 < slots)
                    def _():
                        below_states = take(i + 1, g)
                        give(i, g, [merge(a, b) for a, b in zip(states, below_states)])

                @pl.when(i + 1 >= slots)
                def _():
                    give(i, g, states)
            loop(reached, guest)
            own_below = take(0, g)
            for j in range(GROUP):
                h = g * GROUP + j
                finish(h, merge((acc[:, head_cols(h)], ms[h], ls[h]), own_below[j]))
        loop(chunks, work)

    exchange(0).wait_send()
    exchange(1).wait_send()

    @pl.when(here == 0)
    def _():
        def done(g):
            first_kv(0, g).wait_send()
            first_kv(1, g).wait_send()
        loop(chunks, done)

    @pl.when(here == 1)
    def _():
        def done(g):
            relay(0, g).wait_send()
            relay(1, g).wait_send()
        loop(chunks, done)

    def done(g):
        def back(i):
            send_o(i, g).wait_send()
            send_s(i, g).wait_send()
        loop(reached, back)

        @pl.when(here >= 2)
        def _():
            loop(jnp.minimum(reached + 1, slots), lambda i: send_q(i, g).wait_send())
    loop(chunks, done)


def shards(n, queries, keys, values, bank, seeds, reach):
    length, columns = queries.shape
    heads, refl = seeds.shape[1:]
    width = columns // heads
    chunks = heads // GROUP
    slots = max(1, min(WINDOW, n - 2))
    stat = (slots, chunks, 8, 128 * pl.cdiv(length, 128))
    anywhere = pl.BlockSpec(memory_space=pl.ANY)
    return pl.pallas_call(
        functools.partial(kernel, n, slots),
        out_shape=jax.ShapeDtypeStruct((length, columns), BF16),
        in_specs=[
            anywhere,
            anywhere,
            anywhere,
            pl.BlockSpec(memory_space=pltpu.VMEM),
            pl.BlockSpec(memory_space=pltpu.SMEM),
            pl.BlockSpec(memory_space=pltpu.SMEM),
        ],
        out_specs=pl.BlockSpec(memory_space=pltpu.VMEM),
        scratch_shapes=[
            pltpu.VMEM((length, columns), BF16),
            pltpu.VMEM((2 * length, columns), BF16),
            pltpu.VMEM((2 * length, columns), BF16),
            pltpu.VMEM((2 * length, columns), BF16),
            pltpu.VMEM((2 * length, columns), BF16),
            pltpu.VMEM((heads * refl, width), F32),
            pltpu.VMEM((heads, width, 3 * width), BF16),
            pltpu.VMEM((slots, length, columns), BF16),
            pltpu.VMEM((slots, length, columns), BF16),
            pltpu.VMEM((slots, length, columns), BF16),
            pltpu.VMEM((slots, length, columns), BF16),
            pltpu.VMEM(stat, F32),
            pltpu.VMEM(stat, F32),
            pltpu.VMEM((length, columns), F32),
            pltpu.VMEM((heads, length, 1), F32),
            pltpu.VMEM((heads, length, 1), F32),
            pltpu.SemaphoreType.DMA((3,)),
            pltpu.SemaphoreType.DMA((2,)),
            pltpu.SemaphoreType.DMA((2,)),
            pltpu.SemaphoreType.DMA((2, chunks)),
            pltpu.SemaphoreType.DMA((2, chunks)),
            pltpu.SemaphoreType.DMA((2, chunks)),
            pltpu.SemaphoreType.DMA((2, chunks)),
            pltpu.SemaphoreType.DMA((slots, chunks)),
            pltpu.SemaphoreType.DMA((slots, chunks)),
            pltpu.SemaphoreType.DMA((slots, chunks)),
            pltpu.SemaphoreType.DMA((slots, chunks)),
            pltpu.SemaphoreType.DMA((slots, chunks)),
            pltpu.SemaphoreType.DMA((slots, chunks)),
        ],
        compiler_params=pltpu.CompilerParams(
            collective_id=0, has_side_effects=True, vmem_limit_bytes=56 * 2**20
        ),
    )(queries, keys, values, bank, seeds, reach)


def solution(mesh):
    return jax.shard_map(
        functools.partial(shards, mesh.shape["seq"]),
        mesh=mesh,
        in_specs=(
            P(("parts", "seq", "sub"), "head"),
            P(("parts", "seq", "sub"), "head"),
            P(("parts", "seq", "sub"), "head"),
            P(),
            P("parts", "head", None),
            P(("parts", "head")),
        ),
        out_specs=P(("parts", "seq", "sub"), "head"),
        check_vma=False,
    )
```

time: 720 us -> 61.2 us (0.09); the launches traced: 710 us -> 61 us
  waiting for transfers between devices: 391 us -> 0 us
  matrix products: 185 us -> 0 us
  other arithmetic: 65.3 us -> 0 us
  Pallas kernels: 0 us -> 57.6 us
  local copies, waits for them, and re-layouts: 30.4 us -> 3.39 us
  starting transfers between devices: 21.3 us -> 0 us
  between operations: 14.5 us -> 0.01 us
    ppermute x16 -> x0, waiting for transfers between devices: 390 us -> none  [shifted(): return lax.ppermute(shard, axis, pairs)]
    dot_general x98 -> x0, matrix products: 185 us -> none  [the longest x64 142 us: apply_one(): image = jnp.dot(matrix, vector, precision=lax.Precision.HIGHEST)]
    pallas_call x0 -> x1, Pallas kernels: none -> 57.6 us  [shards(): pl.pallas_call(functools.partial(kernel, n, slots), out_shape=jax.ShapeDt...]
    sub x64 -> x0, other arithmetic: 43.9 us -> none  [apply_one(): return (matrix - factor * jnp.outer(image, vector), None)]
    while x96 -> x0, local copies, waits for them, and re-layouts: 23.9 us -> none
    ppermute x16 -> x0, starting transfers between devices: 21.3 us -> none  [shifted(): return lax.ppermute(shard, axis, pairs)]
    reduce_sum x73 -> x0, other arithmetic: 19.9 us -> none  [the longest x9 12.5 us: attend_block(): total = jnp.sum(exp_terms, axis=-1)]
  transfers between devices with their start and end apart: 18 -> 0, of which waited for: 16 -> 0; matrix products, arithmetic and copies ran while one was open for 34% -> 0% of each run, Pallas kernels for 0% -> 0%
where the time goes in v1:
time: 61.2 us; the launch traced here: 61 us
  Pallas kernels  57.6 us (94%)
  local copies, waits for them, and re-layouts  3.39 us (6%)
    pallas_call x1, Pallas kernels, shards(): pl.pallas_call(functools.partial(kernel, n, slots), out_shape=jax.ShapeDt...  57.6 us
    unnamed x2, local copies, waits for them, and re-layouts  3.39 us

profile of v1, /device:TPU:24, one launch (start us, length us, event | category | flops | bytes accessed | tf_op | source)
XLA Modules:
  0.0 61.0 jit_solution(12127777425142257029)
XLA Ops:
  0.0 1.4 %copy.7.seeds_ref = s32[4,16,8]{2,1,0:T(8,128)} copy(s32[4,16,8]{1,2,0:T(8,128)} %param.10) | data formatting | bytes 4096 | tf_op args[4]
  1.4 57.6 %shard_map.64 = bf16[160,2048]{1,0:T(8,128)(2,1)} custom-call(bf16[160,2048]{1,0:T(8,128)(2,1)} %q_hbm.1, bf16[160,2048]{1,0:T(8,128)(2,1)} %k_hbm.1, bf16[160,2048]{1,0:T(8,128)(2,1)} %v_hbm.1, f32[512,128]{1,0:T(8,128)} %bank_ref.1, s32[4,16,8]{2,1,0:T(8,128)} %copy.7.seeds_ref, s32[16]{0:T(128)} %reach_ref.1), custom_call_target="tpu_custom_call" | custom-call | tf_op jit(solution)/shard_map/pallas_call | solution.py:399
  59.0 2.0 %copy.9 = bf16[160,2048]{1,0:T(8,128)(2,1)} copy(bf16[160,2048]{1,0:T(8,128)(2,1)} %shard_map.64) | data formatting | bytes 1310720

commit v2 on v1

--- a/solution.py
+++ b/solution.py
@@ -9,7 +9,8 @@
 from jax.sharding import PartitionSpec as P
 
 WINDOW = 8
-GROUP = 2
+GROUP = 1
+STACK = 3
 LOW = -1e30
 NT = (((1,), (1,)), ((), ()))
 TN = (((0,), (0,)), ((), ()))
@@ -26,12 +27,12 @@
     return one, two, rest - two
 
 
-def build_transforms(here, bank_ref, seeds_ref, u_ref, t_ref, heads, refl, width):
+def build_transforms(bank_ref, seeds_ref, slot, u_ref, t_ref, heads, refl, width):
     rows = heads * refl
 
     def pick(h, carry):
         for r in range(refl):
-            row = seeds_ref[here, h, r]
+            row = seeds_ref[slot, r, h]
             u_ref[pl.ds(h * refl + r, 1), :] = bank_ref[pl.ds(row, 1), :]
         return carry
 
@@ -66,7 +67,7 @@
             left.astype(BF16), right.astype(BF16), TN, preferred_element_type=F32
         )
         t1, t2, t3 = split3(t)
-        t_ref[h] = jnp.concatenate([t1, t2, t3], axis=1).astype(BF16)
+        t_ref[slot, h] = jnp.concatenate([t1, t2, t3], axis=1).astype(BF16)
 
 
 def rotate(q, t):
@@ -78,7 +79,9 @@
 def block(q, k, v, factor, allowed):
     s = lax.dot_general(q, k, NT, preferred_element_type=F32)
     if allowed is not None:
-        s = jnp.where(allowed, s, LOW)
+        first = jnp.where(allowed, s[: allowed.shape[0]], LOW)
+        rest = s[allowed.shape[0] :]
+        s = jnp.concatenate([first, rest], axis=0) if rest.shape[0] else first
     m = jnp.max(s, axis=1, keepdims=True)
     p = jnp.exp2((s - m) * factor)
     total = jnp.sum(p, axis=1, keepdims=True)
@@ -101,13 +104,13 @@
 
 
 def kernel(
-    n, slots, q_hbm, k_hbm, v_hbm, bank_ref, seeds_ref, reach_ref, out_ref,
-    q_ref, kb, vb, k0, v0, u_ref, t_ref, qr, qs, orx, osx, str_, sts, acc, ms, ls,
-    load_sem, ex_send, ex_recv, kv_send, kv_recv, re_send, re_recv,
+    n, slots, q_hbm, k_hbm, v_hbm, bank_ref, seeds_hbm, reach_ref, out_hbm,
+    q_ref, kb, vb, k0, v0, u_ref, t_ref, qr, qs, orx, osx, str_, sts, acc, ms, ls, pk, out_ref, seeds_ref,
+    load_sem, out_sem, ex_send, ex_recv, kv_send, kv_recv, re_send, re_recv,
     q_send, q_recv, o_send, o_recv, s_send, s_recv,
 ):
     length, columns = q_ref.shape
-    heads, refl = seeds_ref.shape[1:]
+    refl, heads = seeds_ref.shape[1:]
     width = columns // heads
     chunks = heads // GROUP
     wide = GROUP * width
@@ -130,6 +133,9 @@
         pltpu.make_async_copy(q_hbm, q_ref, load_sem.at[0]),
         pltpu.make_async_copy(k_hbm, kb.at[rows, :], load_sem.at[1]),
         pltpu.make_async_copy(v_hbm, vb.at[rows, :], load_sem.at[2]),
+        pltpu.make_async_copy(
+            seeds_hbm.at[jnp.minimum(here + 1, n - 1)], seeds_ref.at[0], load_sem.at[3]),
+        pltpu.make_async_copy(seeds_hbm.at[here], seeds_ref.at[1], load_sem.at[4]),
     ]
     for c in loads:
         c.start()
@@ -171,8 +177,14 @@
 
     def send_q(slot, g):
         return pltpu.make_async_remote_copy(
-            src_ref=qs.at[slot, :, cols(g)], dst_ref=qr.at[slot, :, cols(g)],
+            src_ref=qs.at[jnp.maximum(slot - 1, 0), :, cols(g)], dst_ref=qr.at[slot, :, cols(g)],
             send_sem=q_send.at[slot, g], recv_sem=q_recv.at[slot, g],
+            device_id=below, device_id_type=MESH)
+
+    def send_own(g):
+        return pltpu.make_async_remote_copy(
+            src_ref=q_hbm.at[:, cols(g)], dst_ref=qr.at[0, :, cols(g)],
+            send_sem=q_send.at[0, g], recv_sem=q_recv.at[0, g],
             device_id=below, device_id_type=MESH)
 
     def send_o(slot, g):
@@ -193,9 +205,6 @@
             return carry
         lax.fori_loop(0, count, step, 0)
 
-    exchange(0).start()
-    exchange(1).start()
-
     @pl.when(here == 0)
     def _():
         def go(g):
@@ -203,35 +212,28 @@
             first_kv(1, g).start()
         loop(chunks, go)
 
+    @pl.when(here == n - 1)
+    def _():
+        if n > 2:
+            loop(chunks, lambda g: send_own(g).start())
+
+    @pl.when((here >= 2) & (here < n - 1))
+    def _():
+        send_own(0).start()
+        send_own(1).start()
+
+    exchange(0).start()
+    exchange(1).start()
     for c in loads:
         c.wait()
 
-    @pl.when(here >= 1)
-    def _():
-        build_transforms(here, bank_ref, seeds_ref, u_ref, t_ref, heads, refl, width)
-
-    @pl.when(here >= 2)
-    def _():
-        def walk(g):
-            for j in range(GROUP):
-                h = g * GROUP + j
-                qs[0, :, head_cols(h)] = rotate(q_ref[:, head_cols(h)], t_ref[h])
-            send_q(0, g).start()
-
-            def onward(i):
-                send_q(i, g).wait_recv()
-
-                @pl.when(i + 1 < slots)
-                def _():
-                    for j in range(GROUP):
-                        h = g * GROUP + j
-                        qs[i + 1, :, head_cols(h)] = rotate(qr[i, :, head_cols(h)], t_ref[h])
-                    send_q(i + 1, g).start()
-            loop(reached, onward)
-        loop(chunks, walk)
-
-    exchange(0).wait_recv()
-    exchange(1).wait_recv()
+    @pl.when((here >= 1) & (here < n - 1))
+    def _():
+        build_transforms(bank_ref, seeds_ref, 0, u_ref, t_ref, heads, refl, width)
+
+    @pl.when(here == 1)
+    def _():
+        build_transforms(bank_ref, seeds_ref, 1, u_ref, t_ref, heads, refl, width)
 
     place = half * length + lax.broadcasted_iota(jnp.int32, (length, 2 * length), 0)
     allowed = place >= lax.broadcasted_iota(jnp.int32, (length, 2 * length), 1)
@@ -244,24 +246,39 @@
             acc[:, at] = o
             ms[h] = m
             ls[h] = total
-    loop(chunks, own)
+
+    def write(g):
+        return pltpu.make_async_copy(
+            out_ref.at[:, cols(g)], out_hbm.at[:, cols(g)], out_sem.at[g])
 
     def finish(h, state):
         o, m, total = state
         out_ref[:, head_cols(h)] = (o / total).astype(BF16)
 
-    def give(slot, g, states):
+    def hold(slot, g, states):
         lane = lax.broadcasted_iota(jnp.int32, (length, 128), 1)
         packed = jnp.zeros((length, 128), F32)
         for j, (o, m, total) in enumerate(states):
             osx[slot, :, head_cols(g * GROUP + j)] = (o / jnp.maximum(total, 1.0)).astype(BF16)
             packed = jnp.where(lane == 2 * j, m, packed)
             packed = jnp.where(lane == 2 * j + 1, total, packed)
+        return packed
+
+    def give(slot, g, packed):
         padded = sts.shape[3]
         packed = jnp.concatenate([packed, jnp.zeros((padded - length, 128), F32)], axis=0)
         sts[slot, g] = packed.T[: sts.shape[2]]
         send_o(slot, g).start()
         send_s(slot, g).start()
+
+    def unpack(ref, slot, g, stats):
+        states = []
+        for j in range(GROUP):
+            m = stats[:, 2 * j : 2 * j + 1]
+            total = stats[:, 2 * j + 1 : 2 * j + 2]
+            o = ref[slot, :, head_cols(g * GROUP + j)].astype(F32) * total
+            states.append((o, m, total))
+        return states
 
     def take(slot, g):
         send_o(slot, g).wait_recv()
@@ -270,95 +287,127 @@
         stats = jnp.concatenate(
             [stats, jnp.zeros((128 - stats.shape[0], stats.shape[1]), F32)], axis=0
         ).T[:length]
-        states = []
-        for j in range(GROUP):
-            m = stats[:, 2 * j : 2 * j + 1]
-            total = stats[:, 2 * j + 1 : 2 * j + 2]
-            o = orx[slot, :, head_cols(g * GROUP + j)].astype(F32) * total
-            states.append((o, m, total))
-        return states
+        return unpack(orx, slot, g, stats)
 
     @pl.when(here == 0)
     def _():
+        exchange(0).wait_recv()
+        exchange(1).wait_recv()
+
         def last(g):
+            own(g)
             for j in range(GROUP):
                 h = g * GROUP + j
                 finish(h, (acc[:, head_cols(h)], ms[h], ls[h]))
+            write(g).start()
         loop(chunks, last)
 
     @pl.when(here == 1)
     def _():
-        def pass_on(g):
+        exchange(0).wait_recv()
+        exchange(1).wait_recv()
+        guests = list(range(slots)) if n > 2 else []
+        batches = [([-1] + guests)[i : i + STACK] for i in range(0, 1 + len(guests), STACK)]
+
+        def work(g):
             for i in range(2):
                 first_kv(i, g).wait_recv()
                 relay(i, g).start()
-
-        pass_on(0)
-
-        def work(g):
-            for i in range(2):
-                relay(i, g).wait_recv()
+            for i in guests:
+                send_q(i, g).wait_recv()
+            near = []
             for j in range(GROUP):
                 h = g * GROUP + j
                 at = head_cols(h)
-                w = rotate(q_ref[:, at], t_ref[h])
-                far = gated(block(w, k0[:, at], v0[:, at], factor, None), reach_ref[h] >= 1)
-                finish(h, merge((acc[:, at], ms[h], ls[h]), far))
-
-            @pl.when(g + 1 < chunks)
+                for batch in batches:
+                    w = jnp.concatenate([qr[i, :, at] for i in batch if i >= 0], axis=0) if batch != [-1] else None
+                    if w is not None:
+                        w = rotate(w, t_ref[0, h])
+                    if batch[0] < 0:
+                        w = q_ref[:, at] if w is None else jnp.concatenate([q_ref[:, at], w], axis=0)
+                    state = block(
+                        w, kb[:, at], vb[:, at], factor, allowed if batch[0] < 0 else None
+                    )
+                    near.append((state, rotate(w, t_ref[1, h])))
+            for i in range(2):
+                relay(i, g).wait_recv()
+            ready = {i: [] for i in guests}
+            for j in range(GROUP):
+                h = g * GROUP + j
+                at = head_cols(h)
+                for b, batch in enumerate(batches):
+                    first, w = near[j * len(batches) + b]
+                    second = block(w, k0[:, at], v0[:, at], factor, None)
+                    for e, i in enumerate(batch):
+                        part = slice(e * length, (e + 1) * length)
+                        a = tuple(x[part] for x in first)
+                        z = tuple(x[part] for x in second)
+                        z = gated(z, (reach_ref[h] >= i + 2) & (i + 2 <= WINDOW))
+                        if i < 0:
+                            finish(h, merge(a, z))
+                        else:
+                            ready[i].append(merge(gated(a, reach_ref[h] >= i + 1), z))
+            for i in reversed(guests):
+                give(i, g, hold(i, g, ready[i]))
+            write(g).start()
+        loop(chunks, work)
+
+    @pl.when(here >= 2)
+    def _():
+        def walk(g):
+            @pl.when((here < n - 1) & (g + 2 < chunks))
             def _():
-                pass_on(g + 1)
-
-            def guest(i):
-                if n > 2:
-                    send_q(i, g).wait_recv()
-                    states = []
-                    for j in range(GROUP):
-                        h = g * GROUP + j
-                        at = head_cols(h)
-                        w = qr[i, :, at]
-                        near = gated(
-                            block(w, kb[:, at], vb[:, at], factor, None), reach_ref[h] >= i + 1
-                        )
-                        w = rotate(w, t_ref[h])
-                        far = gated(
-                            block(w, k0[:, at], v0[:, at], factor, None),
-                            (reach_ref[h] >= i + 2) & (i + 2 <= WINDOW),
-                        )
-                        states.append(merge(near, far))
-                    give(i, g, states)
-            loop(reached, guest)
-        loop(chunks, work)
-
-    @pl.when(here >= 2)
-    def _():
-        def work(g):
-            def guest(i):
+                send_own(g + 2).start()
+
+            @pl.when(g == 0)
+            def _():
+                exchange(0).wait_recv()
+                exchange(1).wait_recv()
+
+            def onward(i):
+                send_q(i, g).wait_recv()
+                for j in range(GROUP):
+                    h = g * GROUP + j
+                    qs[i, :, head_cols(h)] = rotate(qr[i, :, head_cols(h)], t_ref[0, h])
+
+                @pl.when(i + 1 < slots)
+                def _():
+                    send_q(i + 1, g).start()
+
                 states = []
                 for j in range(GROUP):
                     h = g * GROUP + j
                     at = head_cols(h)
-                    state = block(qr[i, :, at], kb[:, at], vb[:, at], factor, None)
-                    o, m, total = gated(state, reach_ref[h] >= i + 1)
-                    acc2 = (o, m, total)
-                    states.append(acc2)
-
-                if slots > 1:
-                    @pl.when(i + 1 < slots)
-                    def _():
-                        below_states = take(i + 1, g)
-                        give(i, g, [merge(a, b) for a, b in zip(states, below_states)])
+                    state = block(qs[i, :, at], kb[:, at], vb[:, at], factor, None)
+                    states.append(gated(state, reach_ref[h] >= i + 1))
+                packed = hold(i, g, states)
+                pk[i, g] = packed
 
                 @pl.when(i + 1 >= slots)
                 def _():
-                    give(i, g, states)
+                    give(i, g, packed)
+            loop(reached, onward)
+            own(g)
+        loop(chunks, walk)
+
+        def work(g):
+            def guest(k):
+                i = reached - 1 - k
+
+                @pl.when(i + 1 < slots)
+                def _():
+                    ahead = take(i + 1, g)
+                    mine = unpack(osx, i, g, pk[i, g])
+                    give(i, g, hold(i, g, [merge(a, b) for a, b in zip(mine, ahead)]))
             loop(reached, guest)
-            own_below = take(0, g)
+            ahead = take(0, g)
             for j in range(GROUP):
                 h = g * GROUP + j
-                finish(h, merge((acc[:, head_cols(h)], ms[h], ls[h]), own_below[j]))
+                finish(h, merge((acc[:, head_cols(h)], ms[h], ls[h]), ahead[j]))
+            write(g).start()
         loop(chunks, work)
 
+    loop(chunks, lambda g: write(g).wait())
     exchange(0).wait_send()
     exchange(1).wait_send()
 
@@ -391,10 +440,11 @@
 def shards(n, queries, keys, values, bank, seeds, reach):
     length, columns = queries.shape
     heads, refl = seeds.shape[1:]
+    seeds = jnp.swapaxes(seeds, 1, 2)
     width = columns // heads
     chunks = heads // GROUP
     slots = max(1, min(WINDOW, n - 2))
-    stat = (slots, chunks, 8, 128 * pl.cdiv(length, 128))
+    stat = (slots, chunks, 2 * GROUP, 128 * pl.cdiv(length, 128))
     anywhere = pl.BlockSpec(memory_space=pl.ANY)
     return pl.pallas_call(
         functools.partial(kernel, n, slots),
@@ -404,10 +454,10 @@
             anywhere,
             anywhere,
             pl.BlockSpec(memory_space=pltpu.VMEM),
-            pl.BlockSpec(memory_space=pltpu.SMEM),
+            anywhere,
             pl.BlockSpec(memory_space=pltpu.SMEM),
         ],
-        out_specs=pl.BlockSpec(memory_space=pltpu.VMEM),
+        out_specs=anywhere,
         scratch_shapes=[
             pltpu.VMEM((length, columns), BF16),
             pltpu.VMEM((2 * length, columns), BF16),
@@ -415,7 +465,7 @@
             pltpu.VMEM((2 * length, columns), BF16),
             pltpu.VMEM((2 * length, columns), BF16),
             pltpu.VMEM((heads * refl, width), F32),
-            pltpu.VMEM((heads, width, 3 * width), BF16),
+            pltpu.VMEM((2, heads, width, 3 * width), BF16),
             pltpu.VMEM((slots, length, columns), BF16),
             pltpu.VMEM((slots, length, columns), BF16),
             pltpu.VMEM((slots, length, columns), BF16),
@@ -425,7 +475,11 @@
             pltpu.VMEM((length, columns), F32),
             pltpu.VMEM((heads, length, 1), F32),
             pltpu.VMEM((heads, length, 1), F32),
-            pltpu.SemaphoreType.DMA((3,)),
+            pltpu.VMEM((slots, chunks, length, 128), F32),
+            pltpu.VMEM((length, columns), BF16),
+            pltpu.SMEM((2, refl, heads), jnp.int32),
+            pltpu.SemaphoreType.DMA((5,)),
+            pltpu.SemaphoreType.DMA((chunks,)),
             pltpu.SemaphoreType.DMA((2,)),
             pltpu.SemaphoreType.DMA((2,)),
             pltpu.SemaphoreType.DMA((2, chunks)),

time: 61.2 us -> 51 us (0.83)
  Pallas kernels: 57.6 us -> 48.8 us
  local copies, waits for them, and re-layouts: 3.39 us -> 1.98 us
    pallas_call x1, Pallas kernels: 57.6 us -> 48.8 us  [shards(): pl.pallas_call(functools.partial(kernel, n, slots), out_shape=jax.ShapeDt...]
    unnamed x2 -> x1, local copies, waits for them, and re-layouts: 3.39 us -> 1.98 us
where the time goes in v2:
time: 51 us; the launch traced here: 50.8 us
  Pallas kernels  48.8 us (96%)
  local copies, waits for them, and re-layouts  1.98 us (4%)
    pallas_call x1, Pallas kernels, shards(): pl.pallas_call(functools.partial(kernel, n, slots), out_shape=jax.ShapeDt...  48.8 us
    unnamed x1, local copies, waits for them, and re-layouts  1.98 us

profile of v2, /device:TPU:24, one launch (start us, length us, event | category | flops | bytes accessed | tf_op | source)
XLA Modules:
  0.0 50.8 jit_solution(14686973912816452798)
XLA Ops:
  0.0 48.8 %shard_map.64 = bf16[160,2048]{1,0:T(8,128)(2,1)} custom-call(bf16[160,2048]{1,0:T(8,128)(2,1)} %q_hbm.1, bf16[160,2048]{1,0:T(8,128)(2,1)} %k_hbm.1, bf16[160,2048]{1,0:T(8,128)(2,1)} %v_hbm.1, f32[512,128]{1,0:T(8,128)} %bank_ref.1, s32[4,8,16]{2,1,0:T(8,128)} %bitcast.1, s32[16]{0:T(128)} %reach_ref.1), custom_call_target="tpu_custom_call" | custom-call | tf_op jit(solution)/shard_map/pallas_call | solution.py:449
  48.8 2.0 %copy.8 = bf16[160,2048]{1,0:T(8,128)(2,1)} copy(bf16[160,2048]{1,0:T(8,128)(2,1)} %shard_map.64) | data formatting | bytes 1310720
